TPU v7x, 512 devices: a whole 4x8x8 slice. The times are simulated.
512 devices in a mesh: lag: 16 (over y, x_hi), row: 32 (over z, x_lo, core).
Axes of the slice: x: 4 (x_hi: 2, x_lo: 2; x = x_hi * 2 + x_lo), y: 8, z: 8, core: 2. Of those that a mesh axis runs over, the one named last changes fastest.
Arguments:
- newest: bfloat16 [512, 8192], P('lag', 'row'), may hold values from -6 to 6
- earlier: bfloat16 [15, 8192], P(None, 'row'), may hold values from -6 to 6
- lag_matrices: bfloat16 [16, 8192, 8192], P('lag', 'row'), may hold values from -0.015625 to 0.015625
Outputs:
- forces: float32 [512, 8192], P('lag', 'row')
All inputs are finite; a program needn't handle non-finite values.
Results may differ from a plain program's by a relative error of at most 0.0003.
Values may be sent and summed in bfloat16 or wider, within the bound.
No kernel may reach another device: no remote copies, remote signals or barrier semaphores. Data moves between devices by JAX's collectives and lax.ppermute only.
A program may use at most 64 MiB of HBM per device.

v0:
```python
import jax
import jax.numpy as jnp
from jax import lax
from jax.sharding import PartitionSpec as P


def product(window, matrix):
    return lax.dot_general(
        window, matrix, (((1,), (1,)), ((), ())), preferred_element_type=jnp.float32
    )


def on_device(newest, earlier, lag_matrices):
    lag_index = lax.axis_index("lag")
    matrix = lag_matrices[0]
    own_steps = newest.shape[0]
    earlier_rows = earlier.shape[0]
    wide_newest, wide_earlier = (
        lax.all_gather(newest, "row", axis=1, tiled=True),
        lax.all_gather(earlier, "row", axis=1, tiled=True),
    )
    history = lax.all_gather(wide_newest, "lag", axis=0, tiled=True)
    record = jnp.concatenate([wide_earlier, history], axis=0)
    window = lax.dynamic_slice_in_dim(
        record, jnp.int32(0) + earlier_rows - lag_index, own_steps * lax.axis_size("lag"), 0
    )
    return lax.psum_scatter(product(window, matrix), "lag", scatter_dimension=0, tiled=True)


def solution(mesh):
    in_specs = (P("lag", "row"), P(None, "row"), P("lag", "row", None))
    out_specs = P("lag", "row")
    return jax.shard_map(
        on_device, mesh=mesh, in_specs=in_specs, out_specs=out_specs, check_vma=False
    )
```

profile of v0, /device:TPU:64, one launch (start us, length us, event | category | flops | bytes accessed | tf_op | source)
XLA Modules:
  0.0 406.9 jit_solution(5063151854728555198)
XLA Ops:
  6.5 0.0 all-gather.2.cloned.1.call-start
  6.5 41.6 %all_gather.10 = bf16[32,8192]{1,0:T(8,128)(2,1)} all-gather(bf16[32,256]{1,0:T(8,128)(2,1)} %param.3), channel_id=1, replica_groups=mesh['lag'=16,'row'=32] {'row'}, dimensions={1}, use_global_device_ids=true | all-gather | bytes 540672 | tf_op jit(solution)/shard_map/all_gather | solution.py:19
  48.1 0.0 all-gather.2.cloned.1.call-update
  48.2 0.0 reduce-scatter.2.cloned.1.call-start
  48.2 31.9 %all_gather.9 = bf16[15,8192]{1,0:T(8,128)(2,1)S(1)} all-gather(bf16[15,256]{1,0:T(8,128)(2,1)} %param.4), channel_id=1, replica_groups=mesh['lag'=16,'row'=32] {'row'}, dimensions={1}, use_global_device_ids=true | all-gather | bytes 253440 | tf_op jit(solution)/shard_map/all_gather | solution.py:20
  80.1 107.9 %all-gather.2.cloned.1.call-done = bf16[512,8192]{1,0:T(8,128)(2,1)} async-done(((bf16[32,8192]{1,0:T(8,128)(2,1)}), bf16[512,8192]{1,0:T(8,128)(2,1)}) %all-gather.2.cloned.1.call-update) | async-done | bytes 8388624 | tf_op jit(solution)/shard_map/all_gather | solution.py:22
  188.0 7.8 %fusion.1 = f32[512,256]{1,0:T(8,128)} fusion(s32[]{:T(128)S(6)} %select_n.3, bf16[15,8192]{1,0:T(8,128)(2,1)S(1)} %all_gather.9, bf16[512,8192]{1,0:T(8,128)(2,1)} %all-gather.2.cloned.1.call-done, bf16[1,256,8192]{2,1,0:T(8,128)(2,1)} %param.5), kind=kOutput, calls=%fused_computation.3 | convolution fusion | flops 2164260864 | bytes 13352964 | tf_op jit(solution)/shard_map/dot_general | solution.py:8
  195.8 0.0 reduce-scatter.2.cloned.1.call-update
  195.8 204.2 %reduce-scatter.2.cloned.1.call-done = f32[32,256]{1,0:T(8,128)} async-done(((f32[512,256]{1,0:T(8,128)}), f32[32,256]{1,0:T(8,128)}) %reduce-scatter.2.cloned.1.call-update) | async-done | bytes 32784 | tf_op jit(solution)/shard_map/reduce_scatter | solution.py:27
Async XLA Ops:
  6.5 181.5 %all-gather.2.cloned.1.call-start = ((), (), s32[]{:S(2)}) async-start(), calls=%async_computation.1 | async-start | bytes 8912896 | tf_op jit(solution)/shard_map/all_gather | solution.py:22
  48.2 351.9 %reduce-scatter.2.cloned.1.call-start = ((), (), s32[]{:S(2)}) async-start(), calls=%async_computation.2 | async-start | bytes 557056 | tf_op jit(solution)/shard_map/reduce_scatter | solution.py:27
Sparse Core Ops, SparseCore 0:
  48.3 139.6 all-gather.1
  196.0 204.0 reduce-scatter.1
where the time goes:
time: 407 us
  waiting for transfers between devices  312 us (77%)
  blocking collectives  73.5 us (18%)
  between operations  13.4 us (3%)
  matrix products  7.81 us (2%)
    reduce_scatter x1, waiting for transfers between devices, on_device(): lax.psum_scatter(product(window, matrix), 'lag', scatter_dimension=0, til...  204 us
    all_gather x1, waiting for transfers between devices, on_device(): history = lax.all_gather(wide_newest, 'lag', axis=0, tiled=True)  108 us
    all_gather x1, blocking collectives, on_device(): lax.all_gather(newest, 'row', axis=1, tiled=True)  41.6 us
    all_gather x1, blocking collectives, on_device(): lax.all_gather(earlier, 'row', axis=1, tiled=True)  31.9 us
  transfers between devices with their start and end apart: 2, of which 2 were waited for; matrix products, arithmetic and copies ran while one was open for 0% of the time, Pallas kernels for 0%

commit v1 on v0

v1 whole, which is shorter than its diff:
```python
import jax
import jax.numpy as jnp
from jax import lax
from jax.experimental import pallas as pl
from jax.experimental.pallas import tpu as pltpu
from jax.sharding import Mesh, PartitionSpec as P

AXES = ("yh", "yl", "h", "zh", "zl", "l", "c")
SIZES = (4, 2, 2, 4, 2, 2, 2)
LAG = ("yh", "yl", "h")
ROW = ("zh", "zl", "l", "c")
LIKE = ("yh", "h", "zh")

STEPS = 512
PAD = 16
WIDE = 256
BLOCK = 64
MESSAGE = 72
CHUNKS = 16
LIKES = 32
PACKED = LIKES * BLOCK + 4 * PAD


def device_index(x, y, z, c):
    x, y, z = x % 4, y % 8, z % 8
    return (((y * 2 + x // 2) * 8 + z) * 2 + x % 2) * 2 + c


def cubes():
    groups = []
    for c in range(2):
        for x in range(0, 4, 2):
            for y in range(0, 8, 2):
                for z in range(0, 8, 2):
                    pairs = [sorted((v - c, v - c + 1), key=lambda w: w % 2) for v in (x, y, z)]
                    groups.append(
                        [device_index(i, j, k, c) for i in pairs[0] for j in pairs[1] for k in pairs[2]]
                    )
    return groups


def product_kernel(first_row, history, matrix, out, total):
    for chunk in range(CHUNKS):
        zh, zl, l = chunk // 4, chunk // 2 % 2, chunk % 2

        def part(yl, start, rows):
            return history[l * 4 + yl * 2 + zl, start : start + rows, :]

        halves = []
        for half in range(2):
            rows = [part(half, LIKES * BLOCK + zh * PAD, PAD)]
            for yh in range(4):
                for yl in range(2):
                    for h in range(2):
                        like = (yh * 2 + h) * 4 + zh
                        rows.append(part(yl, like * BLOCK + half * 32, 32))
            halves.append(jnp.concatenate(rows, axis=0))
        term = lax.dot_general(
            jnp.concatenate(halves, axis=1),
            matrix[:, chunk * WIDE : (chunk + 1) * WIDE],
            (((1,), (1,)), ((), ())),
            preferred_element_type=jnp.float32,
        )
        total[...] = term if chunk == 0 else total[...] + term
    rows = STEPS + PAD
    out[...] = pltpu.roll(total[...], rows - first_row[0], 0)[:STEPS]


def product(first_row, history, matrix):
    return pl.pallas_call(
        product_kernel,
        out_shape=jax.ShapeDtypeStruct((STEPS, WIDE), jnp.float32),
        in_specs=[
            pl.BlockSpec(memory_space=pltpu.SMEM),
            pl.BlockSpec(memory_space=pltpu.VMEM),
            pl.BlockSpec(memory_space=pltpu.VMEM),
        ],
        out_specs=pl.BlockSpec(memory_space=pltpu.VMEM),
        scratch_shapes=[pltpu.VMEM((STEPS + PAD, WIDE), jnp.float32)],
        compiler_params=pltpu.CompilerParams(vmem_limit_bytes=40 * 1024 * 1024),
        cost_estimate=pl.CostEstimate(
            flops=2 * (STEPS + PAD) * WIDE * WIDE * CHUNKS, bytes_accessed=7 << 20, transcendentals=0
        ),
    )(first_row, history, matrix)


def on_device(newest, earlier, lag_matrices):
    index = {axis: lax.axis_index(axis) for axis in AXES}
    lag = (index["yh"] * 2 + index["yl"]) * 2 + index["h"]
    core = index["c"]
    swap = [(0, 1), (1, 0)]

    matrix = lag_matrices[0].reshape(WIDE, CHUNKS, 2, WIDE)
    given = lax.dynamic_index_in_dim(matrix, 1 - core, 2, keepdims=False).reshape(WIDE, CHUNKS * WIDE)
    kept = lax.dynamic_index_in_dim(matrix, core, 2, keepdims=False).reshape(WIDE, CHUNKS * WIDE)
    taken = lax.ppermute(given, "c", swap)

    padded = jnp.pad(earlier, ((1, 0), (0, 0)))
    rows = lax.dynamic_slice(padded, ((index["yh"] * 2 + index["h"]) * 2, index["yl"] * 128), (2, 128))
    block = newest.reshape(32, 2, 128).transpose(1, 0, 2).reshape(BLOCK, 128)
    message = jnp.concatenate([block, rows, jnp.zeros((MESSAGE - BLOCK - 2, 128), block.dtype)], axis=0)

    like = lax.all_to_all(jnp.broadcast_to(message[None], (LIKES, MESSAGE, 128)), LIKE, 0, 0, tiled=True)
    before = like[:, BLOCK : BLOCK + 2].reshape(8, 4, 2, 128).transpose(1, 0, 2, 3).reshape(4 * PAD, 128)
    packed = jnp.concatenate([like[:, :BLOCK].reshape(LIKES * BLOCK, 128), before], axis=0)
    history = lax.all_to_all(
        jnp.broadcast_to(packed[None], (8, PACKED, 128)), AXES, 0, 0, tiled=True, axis_index_groups=cubes()
    )

    first_row = (PAD - lag).astype(jnp.int32)[None]
    for_sibling = product(first_row, history, taken)
    from_sibling = lax.ppermute(for_sibling, "c", swap)
    terms = product(first_row, history, kept) + from_sibling
    terms = lax.all_to_all(terms.reshape(16, 32, WIDE), LAG, 0, 0, tiled=True)
    return jnp.sum(terms, axis=0)


def solution(mesh):
    fine = Mesh(mesh.devices.reshape(SIZES), AXES)
    in_specs = (P(LAG, ROW), P(None, ROW), P(LAG, ROW, None))
    return jax.shard_map(on_device, mesh=fine, in_specs=in_specs, out_specs=P(LAG, ROW), check_vma=False)
```

time: 407 us -> 133 us (0.33)
  the two profiles are of different devices: /device:TPU:64 before, /device:TPU:2 now
where the time goes in v1:
time: 133 us; the launch traced here: 132 us
  blocking collectives  66.4 us (50%)
  local copies, waits for them, and re-layouts  43 us (32%)
  starting transfers between devices  9.83 us (7%)
  Pallas kernels  7.41 us (6%)
  waiting for transfers between devices  4.33 us (3%)
    all_to_all x1, blocking collectives, on_device(): lax.all_to_all(jnp.broadcast_to(message[None], (LIKES, MESSAGE, 128)), LI...  41.5 us
    dynamic_slice x1, local copies, waits for them, and re-layouts, on_device(): lax.dynamic_index_in_dim(matrix, 1 - core, 2, keepdims=False)  27.7 us
    all_to_all x1, blocking collectives, on_device(): terms = lax.all_to_all(terms.reshape(16, 32, WIDE), LAG, 0, 0, tiled=True)  24.9 us
    another operation x1, local copies, waits for them, and re-layouts, on_device(): matrix = lag_matrices[0].reshape(WIDE, CHUNKS, 2, WIDE)  7.82 us
    pallas_call x2, Pallas kernels, product(): pl.pallas_call(product_kernel, out_shape=jax.ShapeDtypeStruct((STEPS, WID...  7.41 us
    all_to_all x1, starting transfers between devices, on_device(): lax.all_to_all(jnp.broadcast_to(packed[None], (8, PACKED, 128)), AXES, 0,...  5.88 us
    ppermute x1, waiting for transfers between devices, on_device(): taken = lax.ppermute(given, 'c', swap)  4.33 us
    unnamed x4, local copies, waits for them, and re-layouts  3.25 us
  transfers between devices with their start and end apart: 3, of which 1 were waited for; matrix products, arithmetic and copies ran while one was open for 29% of the time, Pallas kernels for 3%

profile of v1, /device:TPU:2, one launch (start us, length us, event | category | flops | bytes accessed | tf_op | source)
XLA Modules:
  0.0 132.0 jit_solution(7447961108752105677)
XLA Ops:
  0.0 0.7 reshape.28
  0.7 0.1 pad.9.clone
  0.8 0.8 pad_dynamic-slice_fusion
  1.6 0.1 maximum_maximum_fusion
  1.7 0.1 broadcast_in_dim.20
  1.8 41.5 %all_to_all.15 = bf16[32,72,128]{2,1,0:T(8,128)(2,1)S(1)} all-to-all(bf16[32,72,128]{2,1,0:T(8,128)(2,1)S(1)} %broadcast_in_dim.20), channel_id=1, replica_groups=mesh['yh'=4,'yl'=2,'h'=2,'zh'=4,'zl'=2,'l'=2,'c'=2] {'yh','h','zh'}, dimensions={0} | all-to-all | bytes 1179648 | tf_op jit(solution)/shard_map/all_to_all | solution.py:103
  43.3 0.1 slice.8
  43.4 2.6 %broadcast_in_dim.21 = bf16[8,2112,128]{2,1,0:T(8,128)(2,1)} broadcast(bf16[2112,128]{1,0:T(8,128)(2,1)S(1)} %pad_maximum_fusion), dimensions={1,2} | broadcast | bytes 4866048 | tf_op jit(solution)/shard_map/broadcast_in_dim | solution.py:107
  46.0 5.9 %all-to-all-start.1 = ((bf16[8,2112,128]{2,1,0:T(8,128)(2,1)}), bf16[8,2112,128]{2,1,0:T(8,128)(2,1)}, u32[]{:S(2)}, u32[]{:S(2)}) async-start(bf16[8,2112,128]{2,1,0:T(8,128)(2,1)} %broadcast_in_dim.21), calls=%async_computation.1 | async-start | bytes 8650752 | tf_op jit(solution)/shard_map/all_to_all | solution.py:106
  51.8 7.8 %reshape_squeeze.3 = bf16[256,16,2,256]{3,2,1,0:T(2,128)(2,1)} reshape(bf16[1,256,8192]{2,1,0:T(8,128)(2,1)} %param.5) | data formatting | bytes 8388608 | tf_op jit(solution)/shard_map/reshape;squeeze | solution.py:93
  59.7 27.7 %dynamic-slice_reduce_fusion = (bf16[256,16,256]{2,1,0:T(8,128)(2,1)S(1)}, bf16[256,16,256]{2,1,0:T(8,128)(2,1)}) fusion(bf16[256,16,2,256]{3,2,1,0:T(2,128)(2,1)} %reshape_squeeze.3, s32[]{:T(128)S(6)} %select_n.16, s32[]{:T(128)S(6)} %select_n.15), kind=kLoop, calls=%fused_computation | loop fusion | bytes 8388616 | tf_op jit(solution)/shard_map/jit(dynamic_index_in_dim)/dynamic_slice | solution.py:94
  87.3 2.3 %copy.16 = bf16[32,8,16,256]{3,1,2,0:T(8,128)(2,1)} copy(bf16[32,8,16,256]{3,2,1,0:T(8,128)(2,1)S(1)} %bitcast.15) | data formatting | bytes 4194304
  89.6 1.9 %collective-permute-start = (bf16[256,4096]{1,0:T(8,128)(2,1)}, bf16[256,4096]{1,0:T(8,128)(2,1)S(1)}, u32[]{:S(2)}, u32[]{:S(2)}) collective-permute-start(bf16[256,4096]{1,0:T(8,128)(2,1)} %bitcast.12), channel_id=1, source_target_pairs={{0,1},{1,0},{2,3},{3,2},{4,5},{5,4},{6,7},{7,6},{8,9},{9,8},{10,11... | collective-permute-start | bytes 6291464 | tf_op jit(solution)/shard_map/ppermute | solution.py:96
  91.5 4.3 %collective-permute-done.matrix = bf16[256,4096]{1,0:T(8,128)(2,1)S(1)} collective-permute-done((bf16[256,4096]{1,0:T(8,128)(2,1)}, bf16[256,4096]{1,0:T(8,128)(2,1)S(1)}, u32[]{:S(2)}, u32[]{:S(2)}) %collective-permute-start) | collective-permute-done | bytes 2097184 | tf_op jit(solution)/shard_map/ppermute | solution.py:96
  95.9 0.0 all-to-all-done.1.history
  95.9 0.0 copy-start
  95.9 3.8 %shard_map.38 = f32[512,256]{1,0:T(8,128)S(1)} custom-call(s32[1]{0:T(128)} %bitcast.first_row, bf16[8,2112,128]{2,1,0:T(8,128)(2,1)} %all-to-all-done.1.history, bf16[256,4096]{1,0:T(8,128)(2,1)S(1)} %collective-permute-done.matrix), custom_call_target="tpu_custom_call" | custom-call | flops 1107296256 | bytes 7340032 | tf_op jit(solution)/shard_map/pallas_call | solution.py:70
  99.7 2.0 %collective-permute-start.1 = (f32[512,256]{1,0:T(8,128)S(1)}, f32[512,256]{1,0:T(8,128)S(1)}, u32[]{:S(2)}, u32[]{:S(2)}) collective-permute-start(f32[512,256]{1,0:T(8,128)S(1)} %shard_map.38), channel_id=1, source_target_pairs={{0,1},{1,0},{2,3},{3,2},{4,5},{5,4},{6,7},{7,6},{8,9},{9,8},{10,11... | collective-permute-start | bytes 1572872 | tf_op jit(solution)/shard_map/ppermute | solution.py:112
  101.7 0.0 copy-done
  101.7 0.9 copy.15
  102.7 3.6 %shard_map.37 = f32[512,256]{1,0:T(8,128)S(1)} custom-call(s32[1]{0:T(128)} %bitcast.first_row, bf16[8,2112,128]{2,1,0:T(8,128)(2,1)} %all-to-all-done.1.history, bf16[256,4096]{1,0:T(8,128)(2,1)S(1)} %bitcast.13), custom_call_target="tpu_custom_call" | custom-call | flops 1107296256 | bytes 7340032 | tf_op jit(solution)/shard_map/pallas_call | solution.py:70
  106.3 0.0 collective-permute-done.1
  106.3 0.1 add.35
  106.4 24.9 %all_to_all.16 = f32[16,32,256]{2,1,0:T(8,128)S(1)} all-to-all(f32[16,32,256]{2,1,0:T(8,128)S(1)} %bitcast.16), channel_id=1, replica_groups=mesh['yh'=4,'yl'=2,'h'=2,'zh'=4,'zl'=2,'l'=2,'c'=2] {'yh','yl','h'}, dimensions={0} | all-to-all | bytes 1048576 | tf_op jit(solution)/shard_map/all_to_all | solution.py:114
  131.3 0.6 reduce_sum.9
  (6 shorter events, 0.1 us)
Async XLA Ops:
  46.0 49.9 %all-to-all-start.1 = ((bf16[8,2112,128]{2,1,0:T(8,128)(2,1)}), bf16[8,2112,128]{2,1,0:T(8,128)(2,1)}, u32[]{:S(2)}, u32[]{:S(2)}) async-start(bf16[8,2112,128]{2,1,0:T(8,128)(2,1)} %broadcast_in_dim.21), calls=%async_computation.1 | async-start | bytes 8650752 | tf_op jit(solution)/shard_map/all_to_all | solution.py:106
  89.6 6.3 %collective-permute-start = (bf16[256,4096]{1,0:T(8,128)(2,1)}, bf16[256,4096]{1,0:T(8,128)(2,1)S(1)}, u32[]{:S(2)}, u32[]{:S(2)}) collective-permute-start(bf16[256,4096]{1,0:T(8,128)(2,1)} %bitcast.12), channel_id=1, source_target_pairs={{0,1},{1,0},{2,3},{3,2},{4,5},{5,4},{6,7},{7,6},{8,9},{9,8},{10,11... | collective-permute-start | bytes 6291464 | tf_op jit(solution)/shard_map/ppermute | solution.py:96
  95.9 5.8 %copy-start = (bf16[256,16,256]{2,1,0:T(8,128)(2,1)S(1)}, bf16[256,16,256]{2,1,0:T(8,128)(2,1)}, u32[]{:S(2)}) copy-start(bf16[256,16,256]{2,1,0:T(8,128)(2,1)} %get-tuple-element.6) | copy-start | bytes 6291460
  99.7 6.6 %collective-permute-start.1 = (f32[512,256]{1,0:T(8,128)S(1)}, f32[512,256]{1,0:T(8,128)S(1)}, u32[]{:S(2)}, u32[]{:S(2)}) collective-permute-start(f32[512,256]{1,0:T(8,128)S(1)} %shard_map.38), channel_id=1, source_target_pairs={{0,1},{1,0},{2,3},{3,2},{4,5},{5,4},{6,7},{7,6},{8,9},{9,8},{10,11... | collective-permute-start | bytes 1572872 | tf_op jit(solution)/shard_map/ppermute | solution.py:112

commit v2 on v1

--- a/solution.py
+++ b/solution.py
@@ -39,7 +39,12 @@
     return groups
 
 
-def product_kernel(first_row, history, matrix, out, total):
+def lag_index():
+    return (lax.axis_index("yh") * 2 + lax.axis_index("yl")) * 2 + lax.axis_index("h")
+
+
+def product_kernel(history, matrix, out, total):
+    first_row, core = PAD - lag_index(), lax.axis_index("c")
     for chunk in range(CHUNKS):
         zh, zl, l = chunk // 4, chunk // 2 % 2, chunk % 2
 
@@ -57,43 +62,38 @@
             halves.append(jnp.concatenate(rows, axis=0))
         term = lax.dot_general(
             jnp.concatenate(halves, axis=1),
-            matrix[:, chunk * WIDE : (chunk + 1) * WIDE],
+            matrix[:, pl.ds(pl.multiple_of((2 * chunk + core) * WIDE, WIDE), WIDE)],
             (((1,), (1,)), ((), ())),
             preferred_element_type=jnp.float32,
         )
         total[...] = term if chunk == 0 else total[...] + term
     rows = STEPS + PAD
-    out[...] = pltpu.roll(total[...], rows - first_row[0], 0)[:STEPS]
+    out[...] = pltpu.roll(total[...], rows - first_row, 0)[:STEPS]
 
 
-def product(first_row, history, matrix):
+def product(history, matrix):
     return pl.pallas_call(
         product_kernel,
         out_shape=jax.ShapeDtypeStruct((STEPS, WIDE), jnp.float32),
         in_specs=[
-            pl.BlockSpec(memory_space=pltpu.SMEM),
             pl.BlockSpec(memory_space=pltpu.VMEM),
             pl.BlockSpec(memory_space=pltpu.VMEM),
         ],
         out_specs=pl.BlockSpec(memory_space=pltpu.VMEM),
         scratch_shapes=[pltpu.VMEM((STEPS + PAD, WIDE), jnp.float32)],
-        compiler_params=pltpu.CompilerParams(vmem_limit_bytes=40 * 1024 * 1024),
+        compiler_params=pltpu.CompilerParams(vmem_limit_bytes=16 * 1024 * 1024),
         cost_estimate=pl.CostEstimate(
             flops=2 * (STEPS + PAD) * WIDE * WIDE * CHUNKS, bytes_accessed=7 << 20, transcendentals=0
         ),
-    )(first_row, history, matrix)
+    )(history, matrix)
 
 
 def on_device(newest, earlier, lag_matrices):
     index = {axis: lax.axis_index(axis) for axis in AXES}
-    lag = (index["yh"] * 2 + index["yl"]) * 2 + index["h"]
-    core = index["c"]
     swap = [(0, 1), (1, 0)]
 
-    matrix = lag_matrices[0].reshape(WIDE, CHUNKS, 2, WIDE)
-    given = lax.dynamic_index_in_dim(matrix, 1 - core, 2, keepdims=False).reshape(WIDE, CHUNKS * WIDE)
-    kept = lax.dynamic_index_in_dim(matrix, core, 2, keepdims=False).reshape(WIDE, CHUNKS * WIDE)
-    taken = lax.ppermute(given, "c", swap)
+    matrix = lag_matrices[0]
+    sibling_matrix = lax.ppermute(matrix, "c", swap)
 
     padded = jnp.pad(earlier, ((1, 0), (0, 0)))
     rows = lax.dynamic_slice(padded, ((index["yh"] * 2 + index["h"]) * 2, index["yl"] * 128), (2, 128))
@@ -103,14 +103,14 @@
     like = lax.all_to_all(jnp.broadcast_to(message[None], (LIKES, MESSAGE, 128)), LIKE, 0, 0, tiled=True)
     before = like[:, BLOCK : BLOCK + 2].reshape(8, 4, 2, 128).transpose(1, 0, 2, 3).reshape(4 * PAD, 128)
     packed = jnp.concatenate([like[:, :BLOCK].reshape(LIKES * BLOCK, 128), before], axis=0)
+    packed = packed + 0 * sibling_matrix[0, 0]
     history = lax.all_to_all(
         jnp.broadcast_to(packed[None], (8, PACKED, 128)), AXES, 0, 0, tiled=True, axis_index_groups=cubes()
     )
 
-    first_row = (PAD - lag).astype(jnp.int32)[None]
-    for_sibling = product(first_row, history, taken)
+    for_sibling = product(history, sibling_matrix)
     from_sibling = lax.ppermute(for_sibling, "c", swap)
-    terms = product(first_row, history, kept) + from_sibling
+    terms = product(history, matrix) + from_sibling
     terms = lax.all_to_all(terms.reshape(16, 32, WIDE), LAG, 0, 0, tiled=True)
     return jnp.sum(terms, axis=0)
 

time: 133 us -> 114 us (0.86)
  local copies, waits for them, and re-layouts: 43 us -> 3.49 us
  blocking collectives: 66.4 us -> 98.7 us
  starting transfers between devices: 9.83 us -> 3.83 us
  waiting for transfers between devices: 4.33 us -> 0.44 us
  Pallas kernels: 7.41 us -> 5.17 us
    all_to_all x0 -> x1, blocking collectives: none -> 31.2 us  [on_device(): lax.all_to_all(jnp.broadcast_to(packed[None], (8, PACKED, 128)), AXES, 0,...]
    dynamic_slice x1 -> x0, local copies, waits for them, and re-layouts: 27.7 us -> none  [on_device(): lax.dynamic_index_in_dim(matrix, 1 - core, 2, keepdims=False)]
    another operation x1 -> x0, local copies, waits for them, and re-layouts: 7.82 us -> none  [on_device(): matrix = lag_matrices[0].reshape(WIDE, CHUNKS, 2, WIDE)]
    all_to_all x1 -> x0, starting transfers between devices: 5.88 us -> none  [on_device(): lax.all_to_all(jnp.broadcast_to(packed[None], (8, PACKED, 128)), AXES, 0,...]
    ppermute x1, waiting for transfers between devices: 4.33 us -> 0.01 us  [on_device(): sibling_matrix = lax.ppermute(matrix, 'c', swap)]
    unnamed x4 -> x2, local copies, waits for them, and re-layouts: 3.25 us -> 0.01 us
    pallas_call x2, Pallas kernels: 7.41 us -> 5.17 us  [product(): pl.pallas_call(product_kernel, out_shape=jax.ShapeDtypeStruct((STEPS, WID...]
    broadcast_in_dim x1, local copies, waits for them, and re-layouts: 2.56 us -> 0.56 us  [on_device(): jnp.broadcast_to(packed[None], (8, PACKED, 128))]
  transfers between devices with their start and end apart: 3 -> 2, of which waited for: 1 -> 1; matrix products, arithmetic and copies ran while one was open for 29% -> 2% of each run, Pallas kernels for 3% -> 1%
where the time goes in v2:
time: 114 us; the launch traced here: 113 us
  blocking collectives  98.7 us (87%)
  Pallas kernels  5.17 us (5%)
  starting transfers between devices  3.83 us (3%)
  local copies, waits for them, and re-layouts  3.49 us (3%)
    all_to_all x1, blocking collectives, on_device(): lax.all_to_all(jnp.broadcast_to(message[None], (LIKES, MESSAGE, 128)), LI...  42.3 us
    all_to_all x1, blocking collectives, on_device(): lax.all_to_all(jnp.broadcast_to(packed[None], (8, PACKED, 128)), AXES, 0,...  31.2 us
    all_to_all x1, blocking collectives, on_device(): terms = lax.all_to_all(terms.reshape(16, 32, WIDE), LAG, 0, 0, tiled=True)  25.1 us
    pallas_call x2, Pallas kernels, product(): pl.pallas_call(product_kernel, out_shape=jax.ShapeDtypeStruct((STEPS, WID...  5.17 us
  transfers between devices with their start and end apart: 2, of which 1 were waited for; matrix products, arithmetic and copies ran while one was open for 2% of the time, Pallas kernels for 1%

profile of v2, /device:TPU:2, one launch (start us, length us, event | category | flops | bytes accessed | tf_op | source)
XLA Modules:
  0.0 113.3 jit_solution(16891091069229962127)
XLA Ops:
  0.0 1.9 %collective-permute-start = (bf16[256,8192]{1,0:T(8,128)(2,1)}, bf16[256,8192]{1,0:T(8,128)(2,1)}, u32[]{:S(2)}, u32[]{:S(2)}) collective-permute-start(bf16[256,8192]{1,0:T(8,128)(2,1)} %bitcast.10), channel_id=1, source_target_pairs={{0,1},{1,0},{2,3},{3,2},{4,5},{5,4},{6,7},{7,6},{8,9},{9,8},{10,11... | collective-permute-start | bytes 12582920 | tf_op jit(solution)/shard_map/ppermute | solution.py:96
  1.9 0.7 reshape.34
  2.7 0.1 pad.9.clone
  2.8 0.8 pad_dynamic-slice_fusion
  3.5 0.1 maximum_maximum_fusion
  3.6 0.1 broadcast_in_dim.7
  3.7 42.3 %all_to_all.15 = bf16[32,72,128]{2,1,0:T(8,128)(2,1)S(1)} all-to-all(bf16[32,72,128]{2,1,0:T(8,128)(2,1)S(1)} %broadcast_in_dim.7), channel_id=1, replica_groups=mesh['yh'=4,'yl'=2,'h'=2,'zh'=4,'zl'=2,'l'=2,'c'=2] {'yh','h','zh'}, dimensions={0} | all-to-all | bytes 1179648 | tf_op jit(solution)/shard_map/all_to_all | solution.py:103
  46.1 0.1 slice.12
  46.1 0.0 collective-permute-done.matrix
  46.2 1.2 %slice.14 = bf16[1,1]{1,0:T(2,128)(2,1)} slice(bf16[256,8192]{1,0:T(8,128)(2,1)} %collective-permute-done.matrix), slice={[0:1], [0:1]} | slice | bytes 4 | tf_op jit(solution)/shard_map/slice | solution.py:106
  48.0 0.1 maximum_add_fusion
  48.1 0.6 broadcast_in_dim.8
  48.7 31.2 %all_to_all.16.history = bf16[8,2112,128]{2,1,0:T(8,128)(2,1)S(1)} all-to-all(bf16[8,2112,128]{2,1,0:T(8,128)(2,1)S(1)} %broadcast_in_dim.8), channel_id=1, replica_groups={{0,4,64,68,2,6,66,70},{8,12,72,76,10,14,74,78},{16,20,80,84,18,22,82,86..., dimensions={0} | all-to-all | bytes 8650752 | tf_op jit(solution)/shard_map/all_to_all | solution.py:107
  79.9 0.0 copy-start
  79.9 3.7 %shard_map.38 = f32[512,256]{1,0:T(8,128)S(1)} custom-call(bf16[8,2112,128]{2,1,0:T(8,128)(2,1)S(1)} %all_to_all.16.history, bf16[256,8192]{1,0:T(8,128)(2,1)} %collective-permute-done.matrix), custom_call_target="tpu_custom_call" | custom-call | flops 1107296256 | bytes 7340032 | tf_op jit(solution)/shard_map/pallas_call | solution.py:75
  83.6 1.9 %collective-permute-start.1 = (f32[512,256]{1,0:T(8,128)S(1)}, f32[512,256]{1,0:T(8,128)S(1)}, u32[]{:S(2)}, u32[]{:S(2)}) collective-permute-start(f32[512,256]{1,0:T(8,128)S(1)} %shard_map.38), channel_id=1, source_target_pairs={{0,1},{1,0},{2,3},{3,2},{4,5},{5,4},{6,7},{7,6},{8,9},{9,8},{10,11... | collective-permute-start | bytes 1572872 | tf_op jit(solution)/shard_map/ppermute | solution.py:112
  85.5 0.0 copy-done
  85.5 1.4 %shard_map.37 = f32[512,256]{1,0:T(8,128)S(1)} custom-call(bf16[8,2112,128]{2,1,0:T(8,128)(2,1)S(1)} %all_to_all.16.history, bf16[256,8192]{1,0:T(8,128)(2,1)S(1)} %bitcast.11), custom_call_target="tpu_custom_call" | custom-call | flops 1107296256 | bytes 7340032 | tf_op jit(solution)/shard_map/pallas_call | solution.py:75
  87.0 0.4 collective-permute-done.1
  87.4 0.1 add.29
  87.5 25.1 %all_to_all.17 = f32[16,32,256]{2,1,0:T(8,128)S(1)} all-to-all(f32[16,32,256]{2,1,0:T(8,128)S(1)} %bitcast.12), channel_id=1, replica_groups=mesh['yh'=4,'yl'=2,'h'=2,'zh'=4,'zl'=2,'l'=2,'c'=2] {'yh','yl','h'}, dimensions={0} | all-to-all | bytes 1048576 | tf_op jit(solution)/shard_map/all_to_all | solution.py:114
  112.6 0.6 reduce_sum.9
  (5 shorter events, 0.0 us)
Async XLA Ops:
  0.0 46.1 %collective-permute-start = (bf16[256,8192]{1,0:T(8,128)(2,1)}, bf16[256,8192]{1,0:T(8,128)(2,1)}, u32[]{:S(2)}, u32[]{:S(2)}) collective-permute-start(bf16[256,8192]{1,0:T(8,128)(2,1)} %bitcast.10), channel_id=1, source_target_pairs={{0,1},{1,0},{2,3},{3,2},{4,5},{5,4},{6,7},{7,6},{8,9},{9,8},{10,11... | collective-permute-start | bytes 12582920 | tf_op jit(solution)/shard_map/ppermute | solution.py:96
  79.9 5.7 %copy-start = (bf16[1,256,8192]{2,1,0:T(8,128)(2,1)S(1)}, bf16[1,256,8192]{2,1,0:T(8,128)(2,1)}, u32[]{:S(2)}) copy-start(bf16[1,256,8192]{2,1,0:T(8,128)(2,1)} %param.5) | copy-start | bytes 12582916
  83.6 3.8 %collective-permute-start.1 = (f32[512,256]{1,0:T(8,128)S(1)}, f32[512,256]{1,0:T(8,128)S(1)}, u32[]{:S(2)}, u32[]{:S(2)}) collective-permute-start(f32[512,256]{1,0:T(8,128)S(1)} %shard_map.38), channel_id=1, source_target_pairs={{0,1},{1,0},{2,3},{3,2},{4,5},{5,4},{6,7},{7,6},{8,9},{9,8},{10,11... | collective-permute-start | bytes 1572872 | tf_op jit(solution)/shard_map/ppermute | solution.py:112

commit v3 on v2

v3 whole, which is shorter than its diff:
```python
import jax
import jax.numpy as jnp
from jax import lax
from jax.experimental import pallas as pl
from jax.experimental.pallas import tpu as pltpu
from jax.sharding import Mesh, PartitionSpec as P

AXES = ("yh", "yl", "h", "zh", "zl", "l", "c")
SIZES = (4, 2, 2, 4, 2, 2, 2)
LAG = ("yh", "yl", "h")
ROW = ("zh", "zl", "l", "c")

RINGS = (4, 8, 8)
STEPS = 512
OWN = 32
PAD = 16
WIDE = 256
HALF = 128
BLOCK = 64
MESSAGE = 72
CHUNKS = 16
LIKES = 32
PACKED = LIKES * BLOCK + 8 * PAD
VMEM = pl.BlockSpec(memory_space=pltpu.VMEM)


def split_ring(u, size):
    return u // 2, (u % 2 + u // (size // 2)) % 2


def join_ring(pair, side, size):
    return 2 * pair + (side + 2 * pair // (size // 2)) % 2


def device_index(pairs, sides, c):
    x, y, z = ((join_ring(p, s, n) - c) % n for p, s, n in zip(pairs, sides, RINGS))
    return (((y * 2 + x // 2) * 8 + z) * 2 + x % 2) * 2 + c


def groups_of(same_side):
    all_pairs = [(px, py, pz) for py in range(4) for px in range(2) for pz in range(4)]
    all_sides = [(ax, ay, az) for ax in range(2) for ay in range(2) for az in range(2)]
    if same_side:
        return [[device_index(p, s, c) for p in all_pairs] for c in range(2) for s in all_sides]
    return [[device_index(p, s, c) for s in all_sides] for c in range(2) for p in all_pairs]


def lag_index():
    return (lax.axis_index("yh") * 2 + lax.axis_index("yl")) * 2 + lax.axis_index("h")


def columns_of(chunk, core):
    start = (2 * chunk + core) * WIDE
    return pl.ds(start if isinstance(core, int) else pl.multiple_of(start, WIDE), WIDE)


def position():
    c = lax.axis_index("c")
    x = lax.axis_index("h") * 2 + lax.axis_index("l")
    y = lax.axis_index("yh") * 2 + lax.axis_index("yl")
    z = lax.axis_index("zh") * 2 + lax.axis_index("zl")
    return [split_ring((v + c) % n, n) for v, n in zip((x, y, z), RINGS)]


def message_kernel(newest, earlier, out):
    (_, ax), (py, ay), _ = position()
    before = earlier[...].astype(jnp.float32)
    row = lax.broadcasted_iota(jnp.int32, before.shape, 0) + 1
    mine = jnp.sum(jnp.where(row == ax * 8 + ay * 4 + py, before, 0.0), axis=0, keepdims=True)
    place = lax.broadcasted_iota(jnp.int32, (MESSAGE - BLOCK, HALF), 0)
    extra = jnp.where(place == 0, mine[:, :HALF], jnp.where(place == 1, mine[:, HALF:], 0.0))
    block = newest[...]
    out[...] = jnp.concatenate([block[:, :HALF], block[:, HALF:], extra.astype(block.dtype)], axis=0)


def message(newest, earlier):
    return pl.pallas_call(
        message_kernel,
        out_shape=jax.ShapeDtypeStruct((MESSAGE, HALF), newest.dtype),
        in_specs=[VMEM, VMEM],
        out_specs=VMEM,
    )(newest, earlier)


def pack_kernel(like, sibling_matrix, out, sibling_columns, arrived):
    copies = [
        pltpu.make_async_copy(
            sibling_matrix.at[:, columns_of(chunk, lax.axis_index("c"))],
            sibling_columns.at[:, chunk * WIDE : (chunk + 1) * WIDE],
            arrived.at[chunk],
        )
        for chunk in range(CHUNKS)
    ]
    for copy in copies:
        copy.start()
    _, (_, ay), _ = position()
    place = lax.broadcasted_iota(jnp.int32, (PAD, HALF), 0) - ay * 4
    for pz in range(4):
        for px in range(2):
            before = jnp.zeros((PAD, HALF), jnp.float32)
            for py in range(4):
                index = (py * 2 + px) * 4 + pz
                whole = like[index]
                for copy in range(8):
                    out[copy, index * BLOCK : (index + 1) * BLOCK, :] = whole[:BLOCK]
                extra = whole[BLOCK:].astype(jnp.float32)
                before = jnp.where(place == py, extra[0:1], jnp.where(place == 8 + py, extra[1:2], before))
            start = LIKES * BLOCK + (pz * 2 + px) * PAD
            for copy in range(8):
                out[copy, start : start + PAD, :] = before.astype(like.dtype)
    for copy in copies:
        copy.wait()


def pack(like, sibling_matrix):
    return pl.pallas_call(
        pack_kernel,
        out_shape=[
            jax.ShapeDtypeStruct((8, PACKED, HALF), like.dtype),
            jax.ShapeDtypeStruct((WIDE, CHUNKS * WIDE), like.dtype),
        ],
        in_specs=[VMEM, pl.BlockSpec(memory_space=pl.ANY)],
        out_specs=[VMEM, VMEM],
        scratch_shapes=[pltpu.SemaphoreType.DMA((CHUNKS,))],
        compiler_params=pltpu.CompilerParams(vmem_limit_bytes=16 * 1024 * 1024),
    )(like, sibling_matrix)


def add_products(core, whole, history, matrix, total):
    for chunk in range(CHUNKS):
        z, l = chunk // 2, chunk % 2
        pz, az = split_ring((z + core) % 8, 8)
        halves = [[], []]
        before = []
        for h in range(2):
            px, ax = split_ring((2 * h + l + core) % 4, 4)
            start = LIKES * BLOCK + (pz * 2 + px) * PAD
            both = [history[ax * 4 + ay * 2 + az, start : start + PAD, :].astype(jnp.float32) for ay in range(2)]
            before.append((ax, both[0] + both[1]))
        before = [rows for _, rows in sorted(before, key=lambda entry: entry[0])]
        for half in range(2):
            rows = slice(half * 8, half * 8 + 8)
            halves[half].append(jnp.concatenate([before[0][rows], before[1][rows]], axis=0).astype(history.dtype))
        for y in range(8):
            py, ay = split_ring((y + core) % 8, 8)
            for h in range(2):
                px, ax = split_ring((2 * h + l + core) % 4, 4)
                start = ((py * 2 + px) * 4 + pz) * BLOCK
                for half in range(2):
                    first = start + half * OWN
                    halves[half].append(history[ax * 4 + ay * 2 + az, first : first + OWN, :])
        columns = columns_of(chunk, core) if whole else slice(chunk * WIDE, (chunk + 1) * WIDE)
        term = lax.dot_general(
            jnp.concatenate([jnp.concatenate(rows, axis=0) for rows in halves], axis=1),
            matrix[:, columns],
            (((1,), (1,)), ((), ())),
            preferred_element_type=jnp.float32,
        )
        total[...] = term if chunk == 0 else total[...] + term


def product_kernel(whole, history, matrix, out, total):
    for core in range(2):

        @pl.when(lax.axis_index("c") == core)
        def _():
            add_products(core, whole, history, matrix, total)

    rows = STEPS + PAD
    out[...] = pltpu.roll(total[...], rows - PAD + lag_index(), 0)[:STEPS]


def product(history, matrix):
    def kernel(*refs):
        product_kernel(matrix.shape[1] > CHUNKS * WIDE, *refs)

    return pl.pallas_call(
        kernel,
        out_shape=jax.ShapeDtypeStruct((STEPS, WIDE), jnp.float32),
        in_specs=[VMEM, VMEM],
        out_specs=VMEM,
        scratch_shapes=[pltpu.VMEM((STEPS + PAD, WIDE), jnp.float32)],
        compiler_params=pltpu.CompilerParams(vmem_limit_bytes=16 * 1024 * 1024),
        cost_estimate=pl.CostEstimate(
            flops=2 * (STEPS + PAD) * WIDE * WIDE * CHUNKS, bytes_accessed=7 << 20, transcendentals=0
        ),
    )(history, matrix)


def on_device(newest, earlier, lag_matrices):
    swap = [(0, 1), (1, 0)]

    matrix = lag_matrices[0]
    sibling_matrix = lax.ppermute(matrix, "c", swap)

    own = jnp.broadcast_to(message(newest, earlier)[None], (LIKES, MESSAGE, HALF))
    like = lax.all_to_all(own, AXES, 0, 0, tiled=True, axis_index_groups=groups_of(True))
    packed, sibling_columns = pack(like, sibling_matrix)
    history = lax.all_to_all(packed, AXES, 0, 0, tiled=True, axis_index_groups=groups_of(False))

    for_sibling = product(history, sibling_columns)
    from_sibling = lax.ppermute(for_sibling, "c", swap)
    terms = product(history, matrix) + from_sibling
    terms = lax.all_to_all(terms.reshape(16, OWN, WIDE), LAG, 0, 0, tiled=True)
    return jnp.sum(terms, axis=0)


def solution(mesh):
    fine = Mesh(mesh.devices.reshape(SIZES), AXES)
    in_specs = (P(LAG, ROW), P(None, ROW), P(LAG, ROW, None))
    return jax.shard_map(on_device, mesh=fine, in_specs=in_specs, out_specs=P(LAG, ROW), check_vma=False)
```

time: 114 us -> 104 us (0.912)
  blocking collectives: 98.7 us -> 92 us
  local copies, waits for them, and re-layouts: 3.49 us -> 0.8 us
  Pallas kernels: 5.17 us -> 6.35 us
    all_to_all x3, blocking collectives: 98.7 us -> 92 us  [the longest x1 34.9 us: on_device(): lax.all_to_all(own, AXES, 0, 0, tiled=True, axis_index_groups=groups_of(T...]
    slice x4 -> x0, local copies, waits for them, and re-layouts: 1.26 us -> none  [the longest x1 1.18 us: on_device(): packed = packed + 0 * sibling_matrix[0, 0]]
    pallas_call x2 -> x4, Pallas kernels: 5.17 us -> 6.35 us  [the longest x2 3.12 us: product(): pl.pallas_call(kernel, out_shape=jax.ShapeDtypeStruct((STEPS, WIDE), jnp....]
  transfers between devices with their start and end apart: 2 -> 2, of which waited for: 1 -> 1; matrix products, arithmetic and copies ran while one was open for 2% -> 1% of each run, Pallas kernels for 1% -> 3%
where the time goes in v3:
time: 104 us
  blocking collectives  92 us (88%)
  Pallas kernels  6.35 us (6%)
  starting transfers between devices  3.83 us (4%)
    all_to_all x1, blocking collectives, on_device(): lax.all_to_all(own, AXES, 0, 0, tiled=True, axis_index_groups=groups_of(T...  34.9 us
    all_to_all x1, blocking collectives, on_device(): lax.all_to_all(packed, AXES, 0, 0, tiled=True, axis_index_groups=groups_o...  32 us
    all_to_all x1, blocking collectives, on_device(): terms = lax.all_to_all(terms.reshape(16, OWN, WIDE), LAG, 0, 0, tiled=True)  25.2 us
    pallas_call x2, Pallas kernels, product(): pl.pallas_call(kernel, out_shape=jax.ShapeDtypeStruct((STEPS, WIDE), jnp....  3.12 us
  transfers between devices with their start and end apart: 2, of which 1 were waited for; matrix products, arithmetic and copies ran while one was open for 1% of the time, Pallas kernels for 3%

profile of v3, /device:TPU:2, one launch (start us, length us, event | category | flops | bytes accessed | tf_op | source)
XLA Modules:
  0.0 104.1 jit_solution(8493502455293600256)
XLA Ops:
  0.0 1.9 %collective-permute-start = (bf16[256,8192]{1,0:T(8,128)(2,1)}, bf16[256,8192]{1,0:T(8,128)(2,1)}, u32[]{:S(2)}, u32[]{:S(2)}) collective-permute-start(bf16[256,8192]{1,0:T(8,128)(2,1)} %bitcast.2), channel_id=1, source_target_pairs={{0,1},{1,0},{2,3},{3,2},{4,5},{5,4},{6,7},{7,6},{8,9},{9,8},{10,11... | collective-permute-start | bytes 12582920 | tf_op jit(solution)/shard_map/ppermute | solution.py:194
  1.9 1.3 %shard_map.37 = bf16[72,128]{1,0:T(8,128)(2,1)} custom-call(bf16[32,256]{1,0:T(8,128)(2,1)} %newest.1, bf16[15,256]{1,0:T(8,128)(2,1)} %earlier.1), custom_call_target="tpu_custom_call" | custom-call | tf_op jit(solution)/shard_map/pallas_call | solution.py:77
  3.3 0.8 broadcast_in_dim.2
  4.1 34.9 %all_to_all.15.like = bf16[32,72,128]{2,1,0:T(8,128)(2,1)S(1)} all-to-all(bf16[32,72,128]{2,1,0:T(8,128)(2,1)S(1)} %broadcast_in_dim.2), channel_id=1, replica_groups={{0,8,20,28,34,42,54,62,128,136,148,156,162,170,182,190,320,328,340,348,..., dimensions={0} | all-to-all | bytes 1179648 | tf_op jit(solution)/shard_map/all_to_all | solution.py:197
  38.9 0.0 collective-permute-done.sibling_matrix
  38.9 1.9 %shard_map.38 = (bf16[8,2176,128]{2,1,0:T(8,128)(2,1)S(1)}, bf16[256,4096]{1,0:T(8,128)(2,1)S(1)}) custom-call(bf16[32,72,128]{2,1,0:T(8,128)(2,1)S(1)} %all_to_all.15.like, bf16[256,8192]{1,0:T(8,128)(2,1)} %collective-permute-done.sibling_matrix), custom_call_target="tpu_custom_call" | custom-call | tf_op jit(solution)/shard_map/pallas_call | solution.py:116
  40.8 32.0 %all_to_all.16.refs_0_ = bf16[8,2176,128]{2,1,0:T(8,128)(2,1)S(1)} all-to-all(bf16[8,2176,128]{2,1,0:T(8,128)(2,1)S(1)} %get-tuple-element.7), channel_id=1, replica_groups={{0,4,64,68,2,6,66,70},{8,12,72,76,10,14,74,78},{20,16,84,80,22,18,86,82..., dimensions={0} | all-to-all | bytes 8912896 | tf_op jit(solution)/shard_map/all_to_all | solution.py:199
  72.8 0.0 copy-start
  72.8 1.6 %shard_map.40 = f32[512,256]{1,0:T(8,128)S(1)} custom-call(bf16[8,2176,128]{2,1,0:T(8,128)(2,1)S(1)} %all_to_all.16.refs_0_, bf16[256,4096]{1,0:T(8,128)(2,1)S(1)} %get-tuple-element.8.refs_1_), custom_call_target="tpu_custom_call" | custom-call | flops 1107296256 | bytes 7340032 | tf_op jit(solution)/shard_map/pallas_call | solution.py:177
  74.4 1.9 %collective-permute-start.1 = (f32[512,256]{1,0:T(8,128)S(1)}, f32[512,256]{1,0:T(8,128)S(1)}, u32[]{:S(2)}, u32[]{:S(2)}) collective-permute-start(f32[512,256]{1,0:T(8,128)S(1)} %shard_map.40), channel_id=1, source_target_pairs={{0,1},{1,0},{2,3},{3,2},{4,5},{5,4},{6,7},{7,6},{8,9},{9,8},{10,11... | collective-permute-start | bytes 1572872 | tf_op jit(solution)/shard_map/ppermute | solution.py:202
  76.3 0.0 copy-done
  76.3 1.6 %shard_map.39 = f32[512,256]{1,0:T(8,128)S(1)} custom-call(bf16[8,2176,128]{2,1,0:T(8,128)(2,1)S(1)} %all_to_all.16.refs_0_, bf16[256,8192]{1,0:T(8,128)(2,1)S(1)} %bitcast.3), custom_call_target="tpu_custom_call" | custom-call | flops 1107296256 | bytes 7340032 | tf_op jit(solution)/shard_map/pallas_call | solution.py:177
  77.9 0.3 collective-permute-done.1
  78.2 0.1 add.3
  78.2 25.2 %all_to_all.17 = f32[16,32,256]{2,1,0:T(8,128)S(1)} all-to-all(f32[16,32,256]{2,1,0:T(8,128)S(1)} %bitcast.4), channel_id=1, replica_groups=mesh['yh'=4,'yl'=2,'h'=2,'zh'=4,'zl'=2,'l'=2,'c'=2] {'yh','yl','h'}, dimensions={0} | all-to-all | bytes 1048576 | tf_op jit(solution)/shard_map/all_to_all | solution.py:204
  103.4 0.6 reduce_sum.9
Async XLA Ops:
  0.0 38.9 %collective-permute-start = (bf16[256,8192]{1,0:T(8,128)(2,1)}, bf16[256,8192]{1,0:T(8,128)(2,1)}, u32[]{:S(2)}, u32[]{:S(2)}) collective-permute-start(bf16[256,8192]{1,0:T(8,128)(2,1)} %bitcast.2), channel_id=1, source_target_pairs={{0,1},{1,0},{2,3},{3,2},{4,5},{5,4},{6,7},{7,6},{8,9},{9,8},{10,11... | collective-permute-start | bytes 12582920 | tf_op jit(solution)/shard_map/ppermute | solution.py:194
  72.8 3.5 %copy-start = (bf16[1,256,8192]{2,1,0:T(8,128)(2,1)S(1)}, bf16[1,256,8192]{2,1,0:T(8,128)(2,1)}, u32[]{:S(2)}) copy-start(bf16[1,256,8192]{2,1,0:T(8,128)(2,1)} %param.5) | copy-start | bytes 12582916
  74.4 3.8 %collective-permute-start.1 = (f32[512,256]{1,0:T(8,128)S(1)}, f32[512,256]{1,0:T(8,128)S(1)}, u32[]{:S(2)}, u32[]{:S(2)}) collective-permute-start(f32[512,256]{1,0:T(8,128)S(1)} %shard_map.40), channel_id=1, source_target_pairs={{0,1},{1,0},{2,3},{3,2},{4,5},{5,4},{6,7},{7,6},{8,9},{9,8},{10,11... | collective-permute-start | bytes 1572872 | tf_op jit(solution)/shard_map/ppermute | solution.py:202

commit v4 on v3

v4 whole, which is shorter than its diff:
```python
import functools

import jax
import jax.numpy as jnp
from jax import lax
from jax.experimental import pallas as pl
from jax.experimental.pallas import tpu as pltpu
from jax.sharding import Mesh, PartitionSpec as P

AXES = ("yh", "yl", "h", "zh", "zl", "l", "c")
SIZES = (4, 2, 2, 4, 2, 2, 2)
LAG = ("yh", "yl", "h")
ROW = ("zh", "zl", "l", "c")

RINGS = (4, 8, 8)
STEPS = 512
OWN = 32
PAD = 16
WIDE = 256
HALF = 128
BLOCK = 64
MESSAGE = 72
CHUNKS = 16
LIKES = 32
PACKED = LIKES * BLOCK + 4 * PAD
VMEM = pl.BlockSpec(memory_space=pltpu.VMEM)


def split_ring(u, size):
    return u // 2, (u % 2 + u // (size // 2)) % 2


def join_ring(pair, side, size):
    return 2 * pair + (side + 2 * pair // (size // 2)) % 2


def device_index(pairs, sides, c):
    x, y, z = ((join_ring(p, s, n) - c) % n for p, s, n in zip(pairs, sides, RINGS))
    return (((y * 2 + x // 2) * 8 + z) * 2 + x % 2) * 2 + c


def groups_of(same_side):
    all_pairs = [(px, py, pz) for py in range(4) for px in range(2) for pz in range(4)]
    all_sides = [(ax, ay, az) for ax in range(2) for ay in range(2) for az in range(2)]
    if same_side:
        return [[device_index(p, s, c) for p in all_pairs] for c in range(2) for s in all_sides]
    return [[device_index(p, s, c) for s in all_sides] for c in range(2) for p in all_pairs]


def lag_index():
    return (lax.axis_index("yh") * 2 + lax.axis_index("yl")) * 2 + lax.axis_index("h")


def columns_of(chunk, core):
    start = (2 * chunk + core) * WIDE
    return pl.ds(start if isinstance(core, int) else pl.multiple_of(start, WIDE), WIDE)


def position():
    c = lax.axis_index("c")
    x = lax.axis_index("h") * 2 + lax.axis_index("l")
    y = lax.axis_index("yh") * 2 + lax.axis_index("yl")
    z = lax.axis_index("zh") * 2 + lax.axis_index("zl")
    return [split_ring((v + c) % n, n) for v, n in zip((x, y, z), RINGS)]


def message_kernel(newest, earlier, out):
    (_, ax), (py, ay), _ = position()
    before = earlier[...].astype(jnp.float32)
    row = lax.broadcasted_iota(jnp.int32, before.shape, 0) + 1
    mine = jnp.sum(jnp.where(row == ax * 8 + ay * 4 + py, before, 0.0), axis=0, keepdims=True)
    place = lax.broadcasted_iota(jnp.int32, (MESSAGE - BLOCK, HALF), 0)
    extra = jnp.where(place == 0, mine[:, :HALF], jnp.where(place == 1, mine[:, HALF:], 0.0))
    block = newest[...]
    whole = jnp.concatenate([block[:, :HALF], block[:, HALF:], extra.astype(block.dtype)], axis=0)
    for copy in range(LIKES):
        out[copy] = whole


def message(newest, earlier):
    return pl.pallas_call(
        message_kernel,
        out_shape=jax.ShapeDtypeStruct((LIKES, MESSAGE, HALF), newest.dtype),
        in_specs=[VMEM, VMEM],
        out_specs=VMEM,
    )(newest, earlier)


def column_copies(matrix, held, arrived):
    return [
        pltpu.make_async_copy(
            matrix.at[:, columns_of(chunk, lax.axis_index("c"))], held.at[chunk], arrived.at[chunk]
        )
        for chunk in range(CHUNKS)
    ]


def pack_kernel(like, sibling_matrix, out, columns, arrived):
    copies = column_copies(sibling_matrix, columns, arrived)
    for copy in copies:
        copy.start()
    place = lax.broadcasted_iota(jnp.int32, (PAD, HALF), 0)
    for pz in range(4):
        before = jnp.zeros((PAD, HALF), jnp.float32)
        for py in range(4):
            for px in range(2):
                index = (py * 2 + px) * 4 + pz
                whole = like[index]
                for copy in range(8):
                    out[copy, index * BLOCK : (index + 1) * BLOCK, :] = whole[:BLOCK]
                extra = whole[BLOCK:].astype(jnp.float32)
                for half in range(2):
                    before = jnp.where(place == px * 8 + half * 4 + py, extra[half : half + 1], before)
        start = LIKES * BLOCK + pz * PAD
        for copy in range(8):
            out[copy, start : start + PAD, :] = before.astype(like.dtype)
    for copy in copies:
        copy.wait()


def pack(like, sibling_matrix):
    return pl.pallas_call(
        pack_kernel,
        out_shape=[
            jax.ShapeDtypeStruct((8, PACKED, HALF), like.dtype),
            jax.ShapeDtypeStruct((CHUNKS, WIDE, WIDE), like.dtype),
        ],
        in_specs=[VMEM, pl.BlockSpec(memory_space=pl.ANY)],
        out_specs=[VMEM, VMEM],
        scratch_shapes=[pltpu.SemaphoreType.DMA((CHUNKS,))],
        compiler_params=pltpu.CompilerParams(vmem_limit_bytes=16 * 1024 * 1024),
    )(like, sibling_matrix)


def window_chunk(core, history, chunk):
    z, l = chunk // 2, chunk % 2
    pz, az = split_ring((z + core) % 8, 8)
    sides = {}
    for h in range(2):
        px, ax = split_ring((2 * h + l + core) % 4, 4)
        sides[ax] = px
    start = LIKES * BLOCK + pz * PAD
    before = [
        (sides[ax] * 8, history[ax * 4 + ay * 2 + az, start : start + PAD, :].astype(jnp.float32))
        for ax in range(2)
        for ay in range(2)
    ]
    halves = []
    for half in range(2):
        pieces = [rows[first + half * 4 : first + half * 4 + 4] for first, rows in before]
        blocks = [jnp.concatenate(pieces, axis=0).astype(history.dtype)]
        for y in range(8):
            py, ay = split_ring((y + core) % 8, 8)
            for h in range(2):
                px, ax = split_ring((2 * h + l + core) % 4, 4)
                first = ((py * 2 + px) * 4 + pz) * BLOCK + half * OWN
                blocks.append(history[ax * 4 + ay * 2 + az, first : first + OWN, :])
        halves.append(jnp.concatenate(blocks, axis=0))
    return jnp.concatenate(halves, axis=1)


def product_kernel(matrix_chunk, history, matrix, out, total):
    for core in range(2):

        @pl.when(lax.axis_index("c") == core)
        def _():
            for chunk in range(CHUNKS):
                term = lax.dot_general(
                    window_chunk(core, history, chunk),
                    matrix_chunk(matrix, core, chunk),
                    (((1,), (1,)), ((), ())),
                    preferred_element_type=jnp.float32,
                )
                total[...] = term if chunk == 0 else total[...] + term

    rows = STEPS + PAD
    out[...] = pltpu.roll(total[...], rows - PAD + lag_index(), 0)[:STEPS]


def of_block(matrix, core, chunk):
    return matrix[:, columns_of(chunk, core)]


def of_columns(matrix, core, chunk):
    return matrix[chunk]


def product(matrix_chunk, history, matrix):
    return pl.pallas_call(
        functools.partial(product_kernel, matrix_chunk),
        out_shape=jax.ShapeDtypeStruct((STEPS, WIDE), jnp.float32),
        in_specs=[VMEM, VMEM],
        out_specs=VMEM,
        scratch_shapes=[pltpu.VMEM((STEPS + PAD, WIDE), jnp.float32)],
        compiler_params=pltpu.CompilerParams(vmem_limit_bytes=16 * 1024 * 1024),
        cost_estimate=pl.CostEstimate(
            flops=2 * (STEPS + PAD) * WIDE * WIDE * CHUNKS, bytes_accessed=7 << 20, transcendentals=0
        ),
    )(history, matrix)


def on_device(newest, earlier, lag_matrices):
    swap = [(0, 1), (1, 0)]

    matrix = lag_matrices[0]
    sibling_matrix = lax.ppermute(matrix, "c", swap)

    like = lax.all_to_all(message(newest, earlier), AXES, 0, 0, tiled=True, axis_index_groups=groups_of(True))
    packed, sibling_columns = pack(like, sibling_matrix)
    history = lax.all_to_all(packed, AXES, 0, 0, tiled=True, axis_index_groups=groups_of(False))

    for_sibling = product(of_columns, history, sibling_columns)
    from_sibling = lax.ppermute(for_sibling, "c", swap)
    terms = product(of_block, history, matrix) + from_sibling
    terms = lax.all_to_all(terms.reshape(16, OWN, WIDE), LAG, 0, 0, tiled=True)
    return jnp.sum(terms, axis=0)


def solution(mesh):
    fine = Mesh(mesh.devices.reshape(SIZES), AXES)
    in_specs = (P(LAG, ROW), P(None, ROW), P(LAG, ROW, None))
    return jax.shard_map(on_device, mesh=fine, in_specs=in_specs, out_specs=P(LAG, ROW), check_vma=False)
```

time: 104 us -> 104 us (level)
  transfers between devices with their start and end apart: 2 -> 2, of which waited for: 1 -> 1; matrix products, arithmetic and copies ran while one was open for 1% -> 0% of each run, Pallas kernels for 3% -> 3%
where the time goes in v4:
time: 104 us; the launch traced here: 103 us
  blocking collectives  91.7 us (88%)
  Pallas kernels  6.63 us (6%)
  starting transfers between devices  3.83 us (4%)
    all_to_all x1, blocking collectives, on_device(): lax.all_to_all(message(newest, earlier), AXES, 0, 0, tiled=True, axis_ind...  35.1 us
    all_to_all x1, blocking collectives, on_device(): lax.all_to_all(packed, AXES, 0, 0, tiled=True, axis_index_groups=groups_o...  31.3 us
    all_to_all x1, blocking collectives, on_device(): terms = lax.all_to_all(terms.reshape(16, OWN, WIDE), LAG, 0, 0, tiled=True)  25.3 us
    pallas_call x2, Pallas kernels, product(): pl.pallas_call(functools.partial(product_kernel, matrix_chunk), out_shape...  3.12 us
  transfers between devices with their start and end apart: 2, of which 1 were waited for; matrix products, arithmetic and copies ran while one was open for 0% of the time, Pallas kernels for 3%

profile of v4, /device:TPU:2, one launch (start us, length us, event | category | flops | bytes accessed | tf_op | source)
XLA Modules:
  0.0 103.2 jit_solution(15348165150216451530)
XLA Ops:
  0.0 1.9 %collective-permute-start = (bf16[256,8192]{1,0:T(8,128)(2,1)}, bf16[256,8192]{1,0:T(8,128)(2,1)}, u32[]{:S(2)}, u32[]{:S(2)}) collective-permute-start(bf16[256,8192]{1,0:T(8,128)(2,1)} %bitcast.2), channel_id=1, source_target_pairs={{0,1},{1,0},{2,3},{3,2},{4,5},{5,4},{6,7},{7,6},{8,9},{9,8},{10,11... | collective-permute-start | bytes 12582920 | tf_op jit(solution)/shard_map/ppermute | solution.py:206
  1.9 1.6 %shard_map.37 = bf16[32,72,128]{2,1,0:T(8,128)(2,1)} custom-call(bf16[32,256]{1,0:T(8,128)(2,1)} %newest.1, bf16[15,256]{1,0:T(8,128)(2,1)} %earlier.1), custom_call_target="tpu_custom_call" | custom-call | tf_op jit(solution)/shard_map/pallas_call | solution.py:81
  3.5 35.1 %all_to_all.15.like = bf16[32,72,128]{2,1,0:T(8,128)(2,1)S(1)} all-to-all(bf16[32,72,128]{2,1,0:T(8,128)(2,1)} %shard_map.37), channel_id=1, replica_groups={{0,8,20,28,34,42,54,62,128,136,148,156,162,170,182,190,320,328,340,348,..., dimensions={0} | all-to-all | bytes 1179648 | tf_op jit(solution)/shard_map/all_to_all | solution.py:208
  38.6 0.0 collective-permute-done.sibling_matrix
  38.6 1.9 %shard_map.38 = (bf16[8,2112,128]{2,1,0:T(8,128)(2,1)S(1)}, bf16[16,256,256]{2,1,0:T(8,128)(2,1)S(1)}) custom-call(bf16[32,72,128]{2,1,0:T(8,128)(2,1)S(1)} %all_to_all.15.like, bf16[256,8192]{1,0:T(8,128)(2,1)} %collective-permute-done.sibling_matrix), custom_call_target="tpu_custom_call" | custom-call | tf_op jit(solution)/shard_map/pallas_call | solution.py:122
  40.5 31.3 %all_to_all.16.history = bf16[8,2112,128]{2,1,0:T(8,128)(2,1)S(1)} all-to-all(bf16[8,2112,128]{2,1,0:T(8,128)(2,1)S(1)} %get-tuple-element.7), channel_id=1, replica_groups={{0,4,64,68,2,6,66,70},{8,12,72,76,10,14,74,78},{20,16,84,80,22,18,86,82..., dimensions={0} | all-to-all | bytes 8650752 | tf_op jit(solution)/shard_map/all_to_all | solution.py:210
  71.8 0.0 copy-start
  71.8 1.6 %shard_map.40 = f32[512,256]{1,0:T(8,128)S(1)} custom-call(bf16[8,2112,128]{2,1,0:T(8,128)(2,1)S(1)} %all_to_all.16.history, bf16[16,256,256]{2,1,0:T(8,128)(2,1)S(1)} %get-tuple-element.8.matrix), custom_call_target="tpu_custom_call" | custom-call | flops 1107296256 | bytes 7340032 | tf_op jit(solution)/shard_map/pallas_call | solution.py:189
  73.3 1.9 %collective-permute-start.1 = (f32[512,256]{1,0:T(8,128)S(1)}, f32[512,256]{1,0:T(8,128)S(1)}, u32[]{:S(2)}, u32[]{:S(2)}) collective-permute-start(f32[512,256]{1,0:T(8,128)S(1)} %shard_map.40), channel_id=1, source_target_pairs={{0,1},{1,0},{2,3},{3,2},{4,5},{5,4},{6,7},{7,6},{8,9},{9,8},{10,11... | collective-permute-start | bytes 1572872 | tf_op jit(solution)/shard_map/ppermute | solution.py:213
  75.3 0.0 copy-done
  75.3 1.6 %shard_map.39 = f32[512,256]{1,0:T(8,128)S(1)} custom-call(bf16[8,2112,128]{2,1,0:T(8,128)(2,1)S(1)} %all_to_all.16.history, bf16[256,8192]{1,0:T(8,128)(2,1)S(1)} %bitcast.3), custom_call_target="tpu_custom_call" | custom-call | flops 1107296256 | bytes 7340032 | tf_op jit(solution)/shard_map/pallas_call | solution.py:189
  76.8 0.3 collective-permute-done.1
  77.1 0.1 add.3
  77.2 25.3 %all_to_all.17 = f32[16,32,256]{2,1,0:T(8,128)S(1)} all-to-all(f32[16,32,256]{2,1,0:T(8,128)S(1)} %bitcast.4), channel_id=1, replica_groups=mesh['yh'=4,'yl'=2,'h'=2,'zh'=4,'zl'=2,'l'=2,'c'=2] {'yh','yl','h'}, dimensions={0} | all-to-all | bytes 1048576 | tf_op jit(solution)/shard_map/all_to_all | solution.py:215
  102.6 0.6 reduce_sum.9
Async XLA Ops:
  0.0 38.6 %collective-permute-start = (bf16[256,8192]{1,0:T(8,128)(2,1)}, bf16[256,8192]{1,0:T(8,128)(2,1)}, u32[]{:S(2)}, u32[]{:S(2)}) collective-permute-start(bf16[256,8192]{1,0:T(8,128)(2,1)} %bitcast.2), channel_id=1, source_target_pairs={{0,1},{1,0},{2,3},{3,2},{4,5},{5,4},{6,7},{7,6},{8,9},{9,8},{10,11... | collective-permute-start | bytes 12582920 | tf_op jit(solution)/shard_map/ppermute | solution.py:206
  71.8 3.5 %copy-start = (bf16[1,256,8192]{2,1,0:T(8,128)(2,1)S(1)}, bf16[1,256,8192]{2,1,0:T(8,128)(2,1)}, u32[]{:S(2)}) copy-start(bf16[1,256,8192]{2,1,0:T(8,128)(2,1)} %param.5) | copy-start | bytes 12582916
  73.3 3.8 %collective-permute-start.1 = (f32[512,256]{1,0:T(8,128)S(1)}, f32[512,256]{1,0:T(8,128)S(1)}, u32[]{:S(2)}, u32[]{:S(2)}) collective-permute-start(f32[512,256]{1,0:T(8,128)S(1)} %shard_map.40), channel_id=1, source_target_pairs={{0,1},{1,0},{2,3},{3,2},{4,5},{5,4},{6,7},{7,6},{8,9},{9,8},{10,11... | collective-permute-start | bytes 1572872 | tf_op jit(solution)/shard_map/ppermute | solution.py:213

commit v5 on v4

--- a/solution.py
+++ b/solution.py
@@ -1,5 +1,3 @@
-import functools
-
 import jax
 import jax.numpy as jnp
 from jax import lax
@@ -53,7 +51,7 @@
 
 def columns_of(chunk, core):
     start = (2 * chunk + core) * WIDE
-    return pl.ds(start if isinstance(core, int) else pl.multiple_of(start, WIDE), WIDE)
+    return slice(start, start + WIDE)
 
 
 def position():
@@ -83,22 +81,11 @@
         out_shape=jax.ShapeDtypeStruct((LIKES, MESSAGE, HALF), newest.dtype),
         in_specs=[VMEM, VMEM],
         out_specs=VMEM,
+        compiler_params=pltpu.CompilerParams(vmem_limit_bytes=4 * 1024 * 1024),
     )(newest, earlier)
 
 
-def column_copies(matrix, held, arrived):
-    return [
-        pltpu.make_async_copy(
-            matrix.at[:, columns_of(chunk, lax.axis_index("c"))], held.at[chunk], arrived.at[chunk]
-        )
-        for chunk in range(CHUNKS)
-    ]
-
-
-def pack_kernel(like, sibling_matrix, out, columns, arrived):
-    copies = column_copies(sibling_matrix, columns, arrived)
-    for copy in copies:
-        copy.start()
+def pack_kernel(like, sibling_matrix, out):
     place = lax.broadcasted_iota(jnp.int32, (PAD, HALF), 0)
     for pz in range(4):
         before = jnp.zeros((PAD, HALF), jnp.float32)
@@ -114,21 +101,15 @@
         start = LIKES * BLOCK + pz * PAD
         for copy in range(8):
             out[copy, start : start + PAD, :] = before.astype(like.dtype)
-    for copy in copies:
-        copy.wait()
 
 
 def pack(like, sibling_matrix):
     return pl.pallas_call(
         pack_kernel,
-        out_shape=[
-            jax.ShapeDtypeStruct((8, PACKED, HALF), like.dtype),
-            jax.ShapeDtypeStruct((CHUNKS, WIDE, WIDE), like.dtype),
-        ],
+        out_shape=jax.ShapeDtypeStruct((8, PACKED, HALF), like.dtype),
         in_specs=[VMEM, pl.BlockSpec(memory_space=pl.ANY)],
-        out_specs=[VMEM, VMEM],
-        scratch_shapes=[pltpu.SemaphoreType.DMA((CHUNKS,))],
-        compiler_params=pltpu.CompilerParams(vmem_limit_bytes=16 * 1024 * 1024),
+        out_specs=VMEM,
+        compiler_params=pltpu.CompilerParams(vmem_limit_bytes=12 * 1024 * 1024),
     )(like, sibling_matrix)
 
 
@@ -159,7 +140,7 @@
     return jnp.concatenate(halves, axis=1)
 
 
-def product_kernel(matrix_chunk, history, matrix, out, total):
+def product_kernel(history, matrix, out, total):
     for core in range(2):
 
         @pl.when(lax.axis_index("c") == core)
@@ -167,7 +148,7 @@
             for chunk in range(CHUNKS):
                 term = lax.dot_general(
                     window_chunk(core, history, chunk),
-                    matrix_chunk(matrix, core, chunk),
+                    matrix[:, columns_of(chunk, core)],
                     (((1,), (1,)), ((), ())),
                     preferred_element_type=jnp.float32,
                 )
@@ -177,22 +158,14 @@
     out[...] = pltpu.roll(total[...], rows - PAD + lag_index(), 0)[:STEPS]
 
 
-def of_block(matrix, core, chunk):
-    return matrix[:, columns_of(chunk, core)]
-
-
-def of_columns(matrix, core, chunk):
-    return matrix[chunk]
-
-
-def product(matrix_chunk, history, matrix):
+def product(history, matrix):
     return pl.pallas_call(
-        functools.partial(product_kernel, matrix_chunk),
+        product_kernel,
         out_shape=jax.ShapeDtypeStruct((STEPS, WIDE), jnp.float32),
         in_specs=[VMEM, VMEM],
         out_specs=VMEM,
         scratch_shapes=[pltpu.VMEM((STEPS + PAD, WIDE), jnp.float32)],
-        compiler_params=pltpu.CompilerParams(vmem_limit_bytes=16 * 1024 * 1024),
+        compiler_params=pltpu.CompilerParams(vmem_limit_bytes=12 * 1024 * 1024),
         cost_estimate=pl.CostEstimate(
             flops=2 * (STEPS + PAD) * WIDE * WIDE * CHUNKS, bytes_accessed=7 << 20, transcendentals=0
         ),
@@ -206,12 +179,12 @@
     sibling_matrix = lax.ppermute(matrix, "c", swap)
 
     like = lax.all_to_all(message(newest, earlier), AXES, 0, 0, tiled=True, axis_index_groups=groups_of(True))
-    packed, sibling_columns = pack(like, sibling_matrix)
+    packed = pack(like, sibling_matrix)
     history = lax.all_to_all(packed, AXES, 0, 0, tiled=True, axis_index_groups=groups_of(False))
 
-    for_sibling = product(of_columns, history, sibling_columns)
+    for_sibling = product(history, sibling_matrix)
     from_sibling = lax.ppermute(for_sibling, "c", swap)
-    terms = product(of_block, history, matrix) + from_sibling
+    terms = product(history, matrix) + from_sibling
     terms = lax.all_to_all(terms.reshape(16, OWN, WIDE), LAG, 0, 0, tiled=True)
     return jnp.sum(terms, axis=0)
 

time: 104 us -> 102 us (0.981)
  Pallas kernels: 6.63 us -> 3.76 us
  local copies, waits for them, and re-layouts: 0.01 us -> 1.41 us
    pallas_call x1, Pallas kernels: 1.63 us -> 0.08 us  [message(): pl.pallas_call(message_kernel, out_shape=jax.ShapeDtypeStruct((LIKES, MES...]
    unnamed x2 -> x6, local copies, waits for them, and re-layouts: 0.01 us -> 1.41 us
    pallas_call x3, Pallas kernels: 5 us -> 3.68 us  [the longest x2 3.12 us: product(): pl.pallas_call(product_kernel, out_shape=jax.ShapeDtypeStruct((STEPS, WID...]
  transfers between devices with their start and end apart: 2 -> 2, of which waited for: 1 -> 1; matrix products, arithmetic and copies ran while one was open for 0% -> 0% of each run, Pallas kernels for 3% -> 2%
where the time goes in v5:
time: 102 us
  blocking collectives  91.5 us (90%)
  starting transfers between devices  3.83 us (4%)
  Pallas kernels  3.76 us (4%)
  local copies, waits for them, and re-layouts  1.41 us (1%)
    all_to_all x1, blocking collectives, on_device(): lax.all_to_all(message(newest, earlier), AXES, 0, 0, tiled=True, axis_ind...  34.9 us
    all_to_all x1, blocking collectives, on_device(): lax.all_to_all(packed, AXES, 0, 0, tiled=True, axis_index_groups=groups_o...  31.3 us
    all_to_all x1, blocking collectives, on_device(): terms = lax.all_to_all(terms.reshape(16, OWN, WIDE), LAG, 0, 0, tiled=True)  25.4 us
    pallas_call x2, Pallas kernels, product(): pl.pallas_call(product_kernel, out_shape=jax.ShapeDtypeStruct((STEPS, WID...  3.12 us
  transfers between devices with their start and end apart: 2, of which 1 were waited for; matrix products, arithmetic and copies ran while one was open for 0% of the time, Pallas kernels for 2%

profile of v5, /device:TPU:2, one launch (start us, length us, event | category | flops | bytes accessed | tf_op | source)
XLA Modules:
  0.0 101.6 jit_solution(7900074755587108860)
XLA Ops:
  0.0 1.9 %collective-permute-start = (bf16[256,8192]{1,0:T(8,128)(2,1)}, bf16[256,8192]{1,0:T(8,128)(2,1)S(1)}, u32[]{:S(2)}, u32[]{:S(2)}) collective-permute-start(bf16[256,8192]{1,0:T(8,128)(2,1)} %bitcast.2), channel_id=1, source_target_pairs={{0,1},{1,0},{2,3},{3,2},{4,5},{5,4},{6,7},{7,6},{8,9},{9,8},{10,11... | collective-permute-start | bytes 12582920 | tf_op jit(solution)/shard_map/ppermute | solution.py:179
  1.9 0.0 copy-start.1
  1.9 0.7 copy-done.1
  2.6 0.0 copy-start.2
  2.6 0.7 copy-done.2
  3.3 0.1 shard_map.37
  3.4 34.9 %all_to_all.15.like = bf16[32,72,128]{2,1,0:T(8,128)(2,1)S(1)} all-to-all(bf16[32,72,128]{2,1,0:T(8,128)(2,1)S(1)} %shard_map.37), channel_id=1, replica_groups={{0,8,20,28,34,42,54,62,128,136,148,156,162,170,182,190,320,328,340,348,..., dimensions={0} | all-to-all | bytes 1179648 | tf_op jit(solution)/shard_map/all_to_all | solution.py:181
  38.3 0.0 collective-permute-done.sibling_matrix.matrix
  38.3 0.6 shard_map.38
  38.9 31.3 %all_to_all.16.history = bf16[8,2112,128]{2,1,0:T(8,128)(2,1)S(1)} all-to-all(bf16[8,2112,128]{2,1,0:T(8,128)(2,1)S(1)} %shard_map.38), channel_id=1, replica_groups={{0,4,64,68,2,6,66,70},{8,12,72,76,10,14,74,78},{20,16,84,80,22,18,86,82..., dimensions={0} | all-to-all | bytes 8650752 | tf_op jit(solution)/shard_map/all_to_all | solution.py:183
  70.1 0.0 copy-start
  70.1 1.6 %shard_map.40 = f32[512,256]{1,0:T(8,128)S(1)} custom-call(bf16[8,2112,128]{2,1,0:T(8,128)(2,1)S(1)} %all_to_all.16.history, bf16[256,8192]{1,0:T(8,128)(2,1)S(1)} %collective-permute-done.sibling_matrix.matrix), custom_call_target="tpu_custom_call" | custom-call | flops 1107296256 | bytes 7340032 | tf_op jit(solution)/shard_map/pallas_call | solution.py:162
  71.7 1.9 %collective-permute-start.1 = (f32[512,256]{1,0:T(8,128)S(1)}, f32[512,256]{1,0:T(8,128)S(1)}, u32[]{:S(2)}, u32[]{:S(2)}) collective-permute-start(f32[512,256]{1,0:T(8,128)S(1)} %shard_map.40), channel_id=1, source_target_pairs={{0,1},{1,0},{2,3},{3,2},{4,5},{5,4},{6,7},{7,6},{8,9},{9,8},{10,11... | collective-permute-start | bytes 1572872 | tf_op jit(solution)/shard_map/ppermute | solution.py:186
  73.6 0.0 copy-done
  73.6 1.6 %shard_map.39 = f32[512,256]{1,0:T(8,128)S(1)} custom-call(bf16[8,2112,128]{2,1,0:T(8,128)(2,1)S(1)} %all_to_all.16.history, bf16[256,8192]{1,0:T(8,128)(2,1)S(1)} %bitcast.3), custom_call_target="tpu_custom_call" | custom-call | flops 1107296256 | bytes 7340032 | tf_op jit(solution)/shard_map/pallas_call | solution.py:162
  75.2 0.3 collective-permute-done.1
  75.5 0.1 add.3
  75.6 25.4 %all_to_all.17 = f32[16,32,256]{2,1,0:T(8,128)S(1)} all-to-all(f32[16,32,256]{2,1,0:T(8,128)S(1)} %bitcast.4), channel_id=1, replica_groups=mesh['yh'=4,'yl'=2,'h'=2,'zh'=4,'zl'=2,'l'=2,'c'=2] {'yh','yl','h'}, dimensions={0} | all-to-all | bytes 1048576 | tf_op jit(solution)/shard_map/all_to_all | solution.py:188
  100.9 0.6 reduce_sum.9
Async XLA Ops:
  0.0 38.3 %collective-permute-start = (bf16[256,8192]{1,0:T(8,128)(2,1)}, bf16[256,8192]{1,0:T(8,128)(2,1)S(1)}, u32[]{:S(2)}, u32[]{:S(2)}) collective-permute-start(bf16[256,8192]{1,0:T(8,128)(2,1)} %bitcast.2), channel_id=1, source_target_pairs={{0,1},{1,0},{2,3},{3,2},{4,5},{5,4},{6,7},{7,6},{8,9},{9,8},{10,11... | collective-permute-start | bytes 12582920 | tf_op jit(solution)/shard_map/ppermute | solution.py:179
  1.9 0.7 copy-start.1
  2.6 0.7 copy-start.2
  70.1 3.5 %copy-start = (bf16[1,256,8192]{2,1,0:T(8,128)(2,1)S(1)}, bf16[1,256,8192]{2,1,0:T(8,128)(2,1)}, u32[]{:S(2)}) copy-start(bf16[1,256,8192]{2,1,0:T(8,128)(2,1)} %param.5) | copy-start | bytes 12582916
  71.7 3.8 %collective-permute-start.1 = (f32[512,256]{1,0:T(8,128)S(1)}, f32[512,256]{1,0:T(8,128)S(1)}, u32[]{:S(2)}, u32[]{:S(2)}) collective-permute-start(f32[512,256]{1,0:T(8,128)S(1)} %shard_map.40), channel_id=1, source_target_pairs={{0,1},{1,0},{2,3},{3,2},{4,5},{5,4},{6,7},{7,6},{8,9},{9,8},{10,11... | collective-permute-start | bytes 1572872 | tf_op jit(solution)/shard_map/ppermute | solution.py:186

commit v6 on v5

--- a/solution.py
+++ b/solution.py
@@ -145,10 +145,11 @@
 
         @pl.when(lax.axis_index("c") == core)
         def _():
-            for chunk in range(CHUNKS):
+            for chunk in range(0, CHUNKS, 2):
+                both = (chunk, chunk + 1)
                 term = lax.dot_general(
-                    window_chunk(core, history, chunk),
-                    matrix[:, columns_of(chunk, core)],
+                    jnp.concatenate([window_chunk(core, history, k) for k in both], axis=1),
+                    jnp.concatenate([matrix[:, columns_of(k, core)] for k in both], axis=1),
                     (((1,), (1,)), ((), ())),
                     preferred_element_type=jnp.float32,
                 )
@@ -175,10 +176,10 @@
 def on_device(newest, earlier, lag_matrices):
     swap = [(0, 1), (1, 0)]
 
-    matrix = lag_matrices[0]
+    own, matrix = lax.optimization_barrier((message(newest, earlier), lag_matrices[0]))
     sibling_matrix = lax.ppermute(matrix, "c", swap)
 
-    like = lax.all_to_all(message(newest, earlier), AXES, 0, 0, tiled=True, axis_index_groups=groups_of(True))
+    like = lax.all_to_all(own, AXES, 0, 0, tiled=True, axis_index_groups=groups_of(True))
     packed = pack(like, sibling_matrix)
     history = lax.all_to_all(packed, AXES, 0, 0, tiled=True, axis_index_groups=groups_of(False))
 

time: 102 us -> 102 us (level)
  no operation moved by 1% of the time
where the time goes in v6:
time: 102 us
  blocking collectives  91.5 us (90%)
  starting transfers between devices  3.84 us (4%)
  Pallas kernels  3.76 us (4%)
  local copies, waits for them, and re-layouts  1.42 us (1%)
    all_to_all x1, blocking collectives, on_device(): lax.all_to_all(own, AXES, 0, 0, tiled=True, axis_index_groups=groups_of(T...  34.9 us
    all_to_all x1, blocking collectives, on_device(): lax.all_to_all(packed, AXES, 0, 0, tiled=True, axis_index_groups=groups_o...  31.3 us
    all_to_all x1, blocking collectives, on_device(): terms = lax.all_to_all(terms.reshape(16, OWN, WIDE), LAG, 0, 0, tiled=True)  25.4 us
    pallas_call x2, Pallas kernels, product(): pl.pallas_call(product_kernel, out_shape=jax.ShapeDtypeStruct((STEPS, WID...  3.13 us
  transfers between devices with their start and end apart: 2, of which 1 were waited for; matrix products, arithmetic and copies ran while one was open for 0% of the time, Pallas kernels for 2%

profile of v6, /device:TPU:2, one launch (start us, length us, event | category | flops | bytes accessed | tf_op | source)
XLA Modules:
  0.0 101.6 jit_solution(4113146295293761659)
XLA Ops:
  0.0 0.0 copy-start.1
  0.0 0.7 copy-done.1
  0.7 0.0 copy-start.2
  0.7 0.7 copy-done.2
  1.4 0.1 shard_map.37
  1.5 1.9 %collective-permute-start = (bf16[256,8192]{1,0:T(8,128)(2,1)}, bf16[256,8192]{1,0:T(8,128)(2,1)S(1)}, u32[]{:S(2)}, u32[]{:S(2)}) collective-permute-start(bf16[256,8192]{1,0:T(8,128)(2,1)} %bitcast.2), channel_id=1, source_target_pairs={{0,1},{1,0},{2,3},{3,2},{4,5},{5,4},{6,7},{7,6},{8,9},{9,8},{10,11... | collective-permute-start | bytes 12582920 | tf_op jit(solution)/shard_map/ppermute | solution.py:180
  3.4 34.9 %all_to_all.15.like = bf16[32,72,128]{2,1,0:T(8,128)(2,1)S(1)} all-to-all(bf16[32,72,128]{2,1,0:T(8,128)(2,1)S(1)} %shard_map.37), channel_id=1, replica_groups={{0,8,20,28,34,42,54,62,128,136,148,156,162,170,182,190,320,328,340,348,..., dimensions={0} | all-to-all | bytes 1179648 | tf_op jit(solution)/shard_map/all_to_all | solution.py:182
  38.3 0.0 collective-permute-done.sibling_matrix.matrix
  38.3 0.6 shard_map.38
  38.9 31.3 %all_to_all.16.history = bf16[8,2112,128]{2,1,0:T(8,128)(2,1)S(1)} all-to-all(bf16[8,2112,128]{2,1,0:T(8,128)(2,1)S(1)} %shard_map.38), channel_id=1, replica_groups={{0,4,64,68,2,6,66,70},{8,12,72,76,10,14,74,78},{20,16,84,80,22,18,86,82..., dimensions={0} | all-to-all | bytes 8650752 | tf_op jit(solution)/shard_map/all_to_all | solution.py:184
  70.1 0.0 copy-start
  70.1 1.6 %shard_map.40 = f32[512,256]{1,0:T(8,128)S(1)} custom-call(bf16[8,2112,128]{2,1,0:T(8,128)(2,1)S(1)} %all_to_all.16.history, bf16[256,8192]{1,0:T(8,128)(2,1)S(1)} %collective-permute-done.sibling_matrix.matrix), custom_call_target="tpu_custom_call" | custom-call | flops 1107296256 | bytes 7340032 | tf_op jit(solution)/shard_map/pallas_call | solution.py:163
  71.7 1.9 %collective-permute-start.1 = (f32[512,256]{1,0:T(8,128)S(1)}, f32[512,256]{1,0:T(8,128)S(1)}, u32[]{:S(2)}, u32[]{:S(2)}) collective-permute-start(f32[512,256]{1,0:T(8,128)S(1)} %shard_map.40), channel_id=1, source_target_pairs={{0,1},{1,0},{2,3},{3,2},{4,5},{5,4},{6,7},{7,6},{8,9},{9,8},{10,11... | collective-permute-start | bytes 1572872 | tf_op jit(solution)/shard_map/ppermute | solution.py:187
  73.6 0.0 copy-done
  73.6 1.6 %shard_map.39 = f32[512,256]{1,0:T(8,128)S(1)} custom-call(bf16[8,2112,128]{2,1,0:T(8,128)(2,1)S(1)} %all_to_all.16.history, bf16[256,8192]{1,0:T(8,128)(2,1)S(1)} %bitcast.3), custom_call_target="tpu_custom_call" | custom-call | flops 1107296256 | bytes 7340032 | tf_op jit(solution)/shard_map/pallas_call | solution.py:163
  75.2 0.3 collective-permute-done.1
  75.5 0.1 add.3
  75.6 25.4 %all_to_all.17 = f32[16,32,256]{2,1,0:T(8,128)S(1)} all-to-all(f32[16,32,256]{2,1,0:T(8,128)S(1)} %bitcast.4), channel_id=1, replica_groups=mesh['yh'=4,'yl'=2,'h'=2,'zh'=4,'zl'=2,'l'=2,'c'=2] {'yh','yl','h'}, dimensions={0} | all-to-all | bytes 1048576 | tf_op jit(solution)/shard_map/all_to_all | solution.py:189
  100.9 0.6 reduce_sum.9
Async XLA Ops:
  0.0 0.7 copy-start.1
  0.7 0.7 copy-start.2
  1.5 36.8 %collective-permute-start = (bf16[256,8192]{1,0:T(8,128)(2,1)}, bf16[256,8192]{1,0:T(8,128)(2,1)S(1)}, u32[]{:S(2)}, u32[]{:S(2)}) collective-permute-start(bf16[256,8192]{1,0:T(8,128)(2,1)} %bitcast.2), channel_id=1, source_target_pairs={{0,1},{1,0},{2,3},{3,2},{4,5},{5,4},{6,7},{7,6},{8,9},{9,8},{10,11... | collective-permute-start | bytes 12582920 | tf_op jit(solution)/shard_map/ppermute | solution.py:180
  70.1 3.5 %copy-start = (bf16[1,256,8192]{2,1,0:T(8,128)(2,1)S(1)}, bf16[1,256,8192]{2,1,0:T(8,128)(2,1)}, u32[]{:S(2)}) copy-start(bf16[1,256,8192]{2,1,0:T(8,128)(2,1)} %param.5) | copy-start | bytes 12582916
  71.7 3.8 %collective-permute-start.1 = (f32[512,256]{1,0:T(8,128)S(1)}, f32[512,256]{1,0:T(8,128)S(1)}, u32[]{:S(2)}, u32[]{:S(2)}) collective-permute-start(f32[512,256]{1,0:T(8,128)S(1)} %shard_map.40), channel_id=1, source_target_pairs={{0,1},{1,0},{2,3},{3,2},{4,5},{5,4},{6,7},{7,6},{8,9},{9,8},{10,11... | collective-permute-start | bytes 1572872 | tf_op jit(solution)/shard_map/ppermute | solution.py:187
